TPU v7x, 1024 devices: a whole 4x8x16 slice. The times are simulated.
1024 devices in a mesh: row: 64 (over z_hi, x, y), col: 16 (over z_lo, core).
Axes of the slice: x: 4, y: 8, z: 16 (z_hi: 2, z_lo: 8; z = z_hi * 8 + z_lo), core: 2. Of those that a mesh axis runs over, the one named last changes fastest.
Arguments:
- x_start: float32 [8, 131072], P(None, ('row', 'col')), may hold values from -0.75 to 0.75
- p_start: float32 [8, 131072], P(None, ('row', 'col')), may hold values from -0.75 to 0.75
- blocks: bfloat16 [64, 16, 96, 128, 128], P('row', 'col'), may hold values from -0.0546875 to 0.0546875
- block_in_row: int32 [64, 16, 96], P('row', 'col'), may hold values from 0 to 15, as said below
- col_block: int32 [64, 16, 96], P('row', 'col'), may hold values from 0 to 63
- coefs: float32 [2, 24, 8], replicated, may hold values from -3 to 3
Outputs:
- states: float32 [8, 131072], P(None, ('row', 'col'))
Inputs may be any that keep to these rules, and one draw needn't show every extreme that they name: Every stored block lies on or above the block diagonal: col_block * 16 + c >= r * 16 + block_in_row on device (r, c).
All inputs are finite; a program needn't handle non-finite values.
Results may differ from a plain program's by a relative error of at most 0.0034.
Values may be sent and summed in bfloat16 or wider, within the bound.
A program may use at most 32 MiB of HBM per device.

v0:
```python
import jax
import jax.numpy as jnp
from jax import lax
from jax.sharding import PartitionSpec as P

BLOCK = 128
ITERS = 2


def upper_products(left, right):
    return jnp.dot(left, right, precision=lax.Precision.HIGHEST, preferred_element_type=jnp.float32)


def body(x_start, p_start, blocks, block_in_row, col_block, coefs):
    k = x_start.shape[0]
    stored = blocks[0, 0]
    row_of = block_in_row[0, 0]
    col_of = col_block[0, 0]

    def apply_h(vec):
        rows = vec.shape[0]
        low = vec.astype(jnp.bfloat16)
        column_group = lax.all_gather(low, "row", axis=1, tiled=True).reshape(rows, -1, BLOCK)
        row_group = lax.all_gather(low, "col", axis=1, tiled=True).reshape(rows, -1, BLOCK)
        forward = jnp.einsum(
            "mnb,nab->mna", column_group[:, col_of], stored, preferred_element_type=jnp.float32
        )
        lower_products = jnp.einsum(
            "mna,nab->mnb", row_group[:, row_of], stored, preferred_element_type=jnp.float32
        )
        row_hot = (
            row_of[:, None] == jnp.arange(row_group.shape[1], dtype=jnp.int32)[None, :]
        ).astype(jnp.float32)
        column_onehot = (
            col_of[:, None] == jnp.arange(column_group.shape[1], dtype=jnp.int32)[None, :]
        ).astype(jnp.float32)
        row_part = jnp.einsum(
            "mna,nr->mra", forward, row_hot, precision=lax.Precision.HIGHEST
        ).reshape(rows, -1)
        upper = lax.psum_scatter(row_part, "col", scatter_dimension=1, tiled=True)
        col_part = jnp.einsum(
            "fse,sp->fpe", lower_products, column_onehot, precision=lax.Precision.HIGHEST
        ).reshape(rows, -1)
        lower = lax.psum_scatter(col_part, "row", scatter_dimension=1, tiled=True)
        return upper + lower

    both = apply_h(jnp.concatenate([x_start, p_start], 0))
    present_states, direction = (x_start, p_start)
    hx, hp = (both[:k], both[k:])
    zeros_top = jnp.zeros((k, k), jnp.float32)
    for step in range(ITERS):
        quot = lax.psum(upper_products(present_states, hx.T), ("row", "col"))
        resid = hx - upper_products(quot.T, present_states)
        hr = apply_h(resid)
        space = jnp.concatenate([present_states, resid, direction], 0)
        gram = lax.psum(upper_products(space, space.T), ("row", "col"))
        images = jnp.concatenate([hx, hr, hp], 0)
        coef = coefs[step]
        coef_p = jnp.concatenate([zeros_top, coef[k:]], 0)
        norm_x = jnp.diag(upper_products(coef.T, upper_products(gram, coef)))
        norm_p = jnp.diag(upper_products(coef_p.T, upper_products(gram, coef_p)))
        scale_x = 1.0 / jnp.sqrt(norm_x)[:, None]
        scale_p = 1.0 / jnp.sqrt(norm_p)[:, None]
        present_states = upper_products(coef.T, space) * scale_x
        hx = upper_products(coef.T, images) * scale_x
        direction = upper_products(coef_p.T, space) * scale_p
        hp = upper_products(coef_p.T, images) * scale_p
    return present_states


def solution(mesh):
    return jax.shard_map(
        body,
        mesh=mesh,
        in_specs=(
            P(None, ("row", "col")),
            P(None, ("row", "col")),
            P("row", "col", None, None, None),
            P("row", "col", None),
            P("row", "col", None),
            P(),
        ),
        out_specs=P(None, ("row", "col")),
        check_vma=False,
    )
```

profile of v0, /device:TPU:1, one launch (start us, length us, event | category | flops | bytes accessed | tf_op | source)
XLA Modules:
  0.0 2429.1 jit_solution(442028148837447299)
XLA Ops:
  6.5 0.8 convert.6
  7.4 0.8 convert.7
  8.2 285.9 %all_gather.12 = bf16[16,8192]{1,0:T(8,128)(2,1)S(1)} all-gather(bf16[16,128]{1,0:T(8,128)(2,1)S(1)} %pad_maximum_fusion.7), channel_id=1, replica_groups=mesh['row'=64,'col'=16] {'row'}, dimensions={1}, use_global_device_ids=true | all-gather | bytes 266240 | tf_op jit(solution)/shard_map/all_gather | solution.py:23
  294.8 1.4 gather_fusion
  296.2 2.7 fusion.8
  300.3 60.7 %all_gather.13 = bf16[16,2048]{1,0:T(8,128)(2,1)S(1)} all-gather(bf16[16,128]{1,0:T(8,128)(2,1)S(1)} %pad_maximum_fusion.7), channel_id=1, replica_groups=mesh['row'=64,'col'=16] {'col'}, dimensions={1}, use_global_device_ids=true | all-gather | bytes 69632 | tf_op jit(solution)/shard_map/all_gather | solution.py:24
  361.1 1.4 gather_fusion.1
  362.5 1.9 fusion.11
  365.1 1.1 copy.33
  366.4 52.8 %reduce-scatter.5.cloned.1.call-done = f32[16,128]{1,0:T(8,128)} async-done(((f32[16,2048]{1,0:T(8,128)}), f32[16,128]{1,0:T(8,128)}) %reduce-scatter.5.cloned.1.call-update) | async-done | bytes 8208 | tf_op jit(solution)/shard_map/reduce_scatter | solution.py:40
  419.2 554.6 %reduce-scatter.7.cloned.1.call-done = f32[16,128]{1,0:T(8,128)} async-done(((f32[16,8192]{1,0:T(8,128)}), f32[16,128]{1,0:T(8,128)}) %reduce-scatter.7.cloned.1.call-update) | async-done | bytes 8208 | tf_op jit(solution)/shard_map/reduce_scatter | solution.py:44
  973.8 0.7 add.58
  974.7 169.2 %psum.28 = f32[8,8]{0,1:T(8,128)S(1)} all-reduce(f32[8,8]{0,1:T(8,128)S(1)} %convolution_bitcast_fusion.4), channel_id=1, replica_groups=mesh['row'=64,'col'=16] {'row','col'}, use_global_device_ids=true, to_apply=%region_2.0 | all-reduce | flops 64 | bytes 512 | tf_op jit(solution)/shard_map/psum | solution.py:52
  1144.0 28.5 %all_gather.15 = bf16[8,2048]{1,0:T(8,128)(2,1)S(1)} all-gather(bf16[8,128]{1,0:T(8,128)(2,1)S(1)} %get-tuple-element.7), channel_id=1, replica_groups=mesh['row'=64,'col'=16] {'col'}, dimensions={1}, use_global_device_ids=true | all-gather | bytes 34816 | tf_op jit(solution)/shard_map/all_gather | solution.py:24
  1172.5 269.2 %all_gather.14 = bf16[8,8192]{1,0:T(8,128)(2,1)S(1)} all-gather(bf16[8,128]{1,0:T(8,128)(2,1)S(1)} %get-tuple-element.7), channel_id=1, replica_groups=mesh['row'=64,'col'=16] {'row'}, dimensions={1}, use_global_device_ids=true | all-gather | bytes 133120 | tf_op jit(solution)/shard_map/all_gather | solution.py:23
  1442.5 0.9 fusion.17
  1443.7 0.8 copy.34
  1445.2 1.7 fusion.14
  1448.1 143.9 %psum.29 = f32[24,24]{1,0:T(8,128)S(1)} all-reduce(f32[24,24]{1,0:T(8,128)S(1)} %fusion.45), channel_id=1, replica_groups=mesh['row'=64,'col'=16] {'row','col'}, use_global_device_ids=true, to_apply=%region_3.0 | all-reduce | flops 576 | bytes 4608 | tf_op jit(solution)/shard_map/psum | solution.py:56
  1594.3 537.5 %reduce-scatter.11.cloned.1.call-done = f32[8,128]{1,0:T(8,128)} async-done(((f32[8,8192]{1,0:T(8,128)}), f32[8,128]{1,0:T(8,128)}) %reduce-scatter.11.cloned.1.call-update) | async-done | bytes 4112 | tf_op jit(solution)/shard_map/reduce_scatter | solution.py:44
  2131.8 0.7 add.59
  2132.8 169.6 %psum.30 = f32[8,8]{1,0:T(8,128)S(1)} all-reduce(f32[8,8]{1,0:T(8,128)S(1)} %fusion.83), channel_id=1, replica_groups=mesh['row'=64,'col'=16] {'row','col'}, use_global_device_ids=true, to_apply=%region_6.7 | all-reduce | flops 64 | bytes 512 | tf_op jit(solution)/shard_map/psum | solution.py:52
  2302.7 118.2 %psum.31 = f32[24,24]{1,0:T(8,128)S(1)} all-reduce(f32[24,24]{1,0:T(8,128)S(1)} %fusion.41), channel_id=1, replica_groups=mesh['row'=64,'col'=16] {'row','col'}, use_global_device_ids=true, to_apply=%region_7.8 | all-reduce | flops 576 | bytes 4608 | tf_op jit(solution)/shard_map/psum | solution.py:56
  2421.8 0.7 fusion.20
  (60 shorter events, 9.8 us)
Async XLA Ops:
  6.5 289.7 %copy-start = (bf16[1,1,96,128,128]{4,3,2,1,0:T(8,128)(2,1)S(1)}, bf16[1,1,96,128,128]{4,3,2,1,0:T(8,128)(2,1)}, u32[]{:S(2)}) copy-start(bf16[1,1,96,128,128]{4,3,2,1,0:T(8,128)(2,1)} %param.8) | copy-start | bytes 9437188
  6.5 292.4 %copy-start.5 = (s32[1,1,96]{2,1,0:T(1,128)S(1)}, s32[1,1,96]{2,1,0:T(1,128)}, u32[]{:S(2)}) copy-start(s32[1,1,96]{2,1,0:T(1,128)} %param.9) | copy-start | bytes 1156
  6.5 412.6 %reduce-scatter.5.cloned.1.call-start = ((), (), s32[]{:S(2)}) async-start(), calls=%async_computation.4 | async-start | bytes 139264 | tf_op jit(solution)/shard_map/reduce_scatter | solution.py:40
  298.9 65.5 %copy-start.4 = (s32[1,1,96]{2,1,0:T(1,128)S(1)}, s32[1,1,96]{2,1,0:T(1,128)}, u32[]{:S(2)}) copy-start(s32[1,1,96]{2,1,0:T(1,128)} %param.10) | copy-start | bytes 1156
  300.2 673.6 %reduce-scatter.7.cloned.1.call-start = ((), (), s32[]{:S(2)}) async-start(), calls=%async_computation.5 | async-start | bytes 532480 | tf_op jit(solution)/shard_map/reduce_scatter | solution.py:44
  362.5 3.8 copy-start.2
  362.5 612.1 %copy-start.1 = (f32[8,128]{1,0:T(8,128)S(1)}, f32[8,128]{1,0:T(8,128)}, u32[]{:S(2)}) copy-start(f32[8,128]{1,0:T(8,128)} %param.6) | copy-start | bytes 12292
  366.2 1228.1 %reduce-scatter.9.cloned.1.call-start = ((), (), s32[]{:S(2)}) async-start(), calls=%async_computation.6 | async-start | bytes 69632 | tf_op jit(solution)/shard_map/reduce_scatter | solution.py:40
  1443.4 4.6 copy-start.3
  1447.9 683.9 %reduce-scatter.11.cloned.1.call-start = ((), (), s32[]{:S(2)}) async-start(), calls=%async_computation.7 | async-start | bytes 266240 | tf_op jit(solution)/shard_map/reduce_scatter | solution.py:44
Sparse Core Ops, SparseCore 0:
  300.4 118.7 reduce-scatter.4
  422.9 550.8 reduce-scatter.6
  1448.0 114.7 reduce-scatter.8
  1593.5 538.2 reduce-scatter.10
where the time goes:
time: 2430 us
  blocking collectives  1250 us (51%)
  waiting for transfers between devices  1150 us (47%)
    reduce_scatter x2, waiting for transfers between devices, apply_h(): lower = lax.psum_scatter(col_part, 'row', scatter_dimension=1, tiled=True)  1090 us
    all_gather x2, blocking collectives, apply_h(): lax.all_gather(low, 'row', axis=1, tiled=True).reshape(rows, -1, BLOCK)  555 us
    psum x2, blocking collectives, body(): quot = lax.psum(upper_products(present_states, hx.T), ('row', 'col'))  339 us
    psum x2, blocking collectives, body(): gram = lax.psum(upper_products(space, space.T), ('row', 'col'))  262 us
    all_gather x2, blocking collectives, apply_h(): lax.all_gather(low, 'col', axis=1, tiled=True).reshape(rows, -1, BLOCK)  89.3 us
    reduce_scatter x2, waiting for transfers between devices, apply_h(): upper = lax.psum_scatter(row_part, 'col', scatter_dimension=1, tiled=True)  52.8 us
  transfers between devices with their start and end apart: 4, of which 3 were waited for; matrix products, arithmetic and copies ran while one was open for 0% of the time, Pallas kernels for 0%

commit v1 on v0

v1 whole, which is shorter than its diff:
```python
import jax
import jax.numpy as jnp
from jax import lax
from jax.experimental import pallas as pl
from jax.experimental.pallas import tpu as pltpu
from jax.sharding import PartitionSpec as P

MESH = pl.DeviceIdType.MESH
HI = lax.Precision.HIGHEST
F32, BF16 = jnp.float32, jnp.bfloat16
NNZ = 96
PLANE = 32
NCOL = 16
ZLOW = NCOL // 2
ZALL = 2 * ZLOW
UNROLL = 8
NSEM = 48


def dot(a, b, dims, precision=None):
    return lax.dot_general(a, b, (dims, ((), ())), precision=precision, preferred_element_type=F32)


def sort_meta(key_row, other_row, pad_ref):
    lane = lax.broadcasted_iota(jnp.int32, (128, 128), 1).astype(F32)
    sub = lax.broadcasted_iota(jnp.int32, (128, 128), 0).astype(F32)
    pad_ref[...] = jnp.full((8, 128), 1000.0, F32)
    pad_ref[0:1, 0:NNZ] = key_row.astype(F32)
    pad_ref[1:2, 0:NNZ] = other_row.astype(F32)
    key_lane = jnp.broadcast_to(pad_ref[0:1, :], (128, 128))
    other_lane = jnp.broadcast_to(pad_ref[1:2, :], (128, 128))
    key_sub = key_lane.T
    other_sub = other_lane.T
    before = (key_lane < key_sub) | ((key_lane == key_sub) & (lane < sub))
    rank = jnp.sum(jnp.where(before, 1.0, 0.0), axis=1, keepdims=True)
    here = rank == lane
    place = jnp.sum(jnp.where(here, sub, 0.0), axis=0, keepdims=True)
    other = jnp.sum(jnp.where(here, other_sub, 0.0), axis=0, keepdims=True)
    key = jnp.sum(jnp.where(here, key_sub, 0.0), axis=0, keepdims=True)
    earlier = jnp.sum(jnp.where(rank == lane - 1.0, key_sub, 0.0), axis=0, keepdims=True)
    keep = jnp.where(key == earlier, 1.0, 0.0)
    end = jnp.sum(jnp.where(key_sub <= lane, 1.0, 0.0), axis=0, keepdims=True)
    start = jnp.sum(jnp.where(key_sub < lane, 1.0, 0.0), axis=0, keepdims=True)
    last = jnp.where(end > start, end, 0.0)
    return [v.astype(jnp.int32) for v in (place, other, keep, last)]


def gram_tile(basis):
    padded = jnp.concatenate([basis, jnp.zeros((104, 128), F32)], 0)
    g = dot(basis, padded, ((1,), (1,)), HI)
    return g[0:8] + pltpu.roll(g[8:16], 32, 1) + pltpu.roll(g[16:24], 64, 1)


def prepare(row_ref, col_ref, coef_ref, meta_ref, turn_ref, pad_ref):
    rows = row_ref[0]
    cols = col_ref[0]
    for i, v in enumerate(sort_meta(cols, rows, pad_ref) + sort_meta(rows, cols, pad_ref)):
        meta_ref[i:i + 1, :] = v
    k = lax.broadcasted_iota(jnp.int32, (24, 128), 0)
    lane = lax.broadcasted_iota(jnp.int32, (24, 128), 1)
    place = jnp.where(k < 8, k, jnp.where(k < 16, k + 8, k - 8))
    for i in range(2):
        turn_ref[i, 0] = dot(coef_ref[i], jnp.where(lane == place, 1.0, 0.0).astype(F32), ((0,), (0,)), HI)
        only = (lane == k - 8) & (k >= 8) & (k < 16)
        turn_ref[i, 1] = dot(coef_ref[i], jnp.where(only, 1.0, 0.0).astype(F32), ((0,), (0,)), HI)


def rotation(ct, cb, tile):
    lane8 = lax.broadcasted_iota(jnp.int32, (8, 128), 1)
    hx_rows = pltpu.roll(tile, 64, 1)
    at = jnp.where(lane8 < 8, hx_rows, 0.0)
    back = dot(cb[:, 0:8], at, ((1,), (0,)), HI)
    t = ct - back
    tp = jnp.where(lane8 < 8, 0.0, ct) - back
    gam = jnp.concatenate([tile, pltpu.roll(tile, 96, 1), hx_rows], 0)
    both = jnp.concatenate([t, tp], 0)
    norm = jnp.sum(dot(both[:, 0:24], gam, ((1,), (0,)), HI) * both, axis=1, keepdims=True)
    return both, 1.0 / jnp.sqrt(norm)


def kernel(x_ref, p_ref, blk_hbm, meta, turn_ref, o_ref,
           blk, vs, vr1, vr2, vc1, vc2, prefix, cp1, cp2, rp1, rp2, rs1, rs2, cr1, cr2, zs, zr,
           gs, gr, gp, gz, sems):
    r = lax.axis_index("row")
    c = lax.axis_index("col")
    zh = r // PLANE
    p = lax.rem(r, PLANE)
    zl = c // 2
    core = lax.rem(c, 2)
    zi = zh * ZLOW + zl
    other_core = zl * 2 + 1 - core
    other_r = (1 - zh) * PLANE + p

    def copy(src, dst, send, recv, dev):
        return pltpu.make_async_remote_copy(
            src_ref=src, dst_ref=dst, send_sem=sems.at[send], recv_sem=sems.at[recv], device_id=dev, device_id_type=MESH
        )

    def arrived(ref, sem):
        copy(ref, ref, NSEM - 1, sem, (r, other_core)).wait_recv()

    def left(ref, sem):
        copy(ref, ref, sem, NSEM - 1, (r, other_core)).wait_send()

    def plane_send(src, dst, send, recv):
        def step(i, _):
            q = lax.rem(p + i, PLANE)
            copy(src(q), dst, send, recv, (zh * PLANE + q, c)).start()
            return 0

        lax.fori_loop(1, PLANE, step, 0)

    def col_send(src, dst, send, recv):
        def step(i, _):
            q = lax.rem(c + i, NCOL)
            copy(src(q), dst, send, recv, (r, q)).start()
            return 0

        lax.fori_loop(1, NCOL, step, 0)

    def z_send(src, dst, send, recv):
        def step(i, _):
            q = lax.rem(zi + i, ZALL)
            copy(src, dst, send, recv, (q // ZLOW * PLANE + p, lax.rem(q, ZLOW) * 2 + core)).start()
            return 0

        lax.fori_loop(1, ZALL, step, 0)

    bar = pltpu.get_barrier_semaphore()

    def greet_plane(i, _):
        pl.semaphore_signal(bar, 1, device_id=(zh * PLANE + lax.rem(p + i, PLANE), c), device_id_type=MESH)
        return 0

    def greet_col(i, _):
        pl.semaphore_signal(bar, 1, device_id=(r, lax.rem(c + i, NCOL)), device_id_type=MESH)
        return 0

    def greet_far(i, _):
        pl.semaphore_signal(bar, 1, device_id=(other_r, i * 2 + core), device_id_type=MESH)
        return 0

    lax.fori_loop(0, ZLOW, greet_far, 0)
    lax.fori_loop(1, NCOL, greet_col, 0)
    lax.fori_loop(1, PLANE, greet_plane, 0)

    load = pltpu.make_async_copy(blk_hbm.at[0, 0], blk, sems.at[0])
    load.start()
    x = x_ref[...]
    d = p_ref[...]
    vs[0] = jnp.concatenate([x, d], 0).astype(BF16)

    @pl.when(zh == 1)
    def _():
        vc1[0:PLANE] = jnp.zeros((PLANE, 16, 128), BF16)
        vc2[0:PLANE] = jnp.zeros((PLANE, 16, 128), BF16)

    prefix[0] = jnp.zeros((16, 128), F32)
    pl.semaphore_wait(bar, PLANE - 1 + NCOL - 1 + ZLOW)

    def products(v_ref, base, transposed, half):
        dims = ((1,), (1,)) if transposed else ((1,), (0,))
        m = 8 if half else 16

        def step(it, total):
            for u in range(UNROLL):
                k = it * UNROLL + u
                part = dot(v_ref[meta[base + 1, k]], blk[meta[base, k]], dims)
                if half:
                    part = part[0:8] + part[8:16]
                total = total * meta[base + 2, k].astype(F32) + part
                prefix[k + 1, 0:m] = total
            return total

        lax.fori_loop(0, NNZ // UNROLL, step, jnp.zeros((m, 128), F32))

    def apply_h(ph, sem, hooks):
        half = ph == 1
        v = vs.at[ph]
        vr, vc = (vr2, vc2) if half else (vr1, vc1)

        @pl.when(zh == 1)
        def _():
            copy(v, vc.at[r], sem + 1, sem, (p, c)).start()

        col_send(lambda q: v, vr.at[c], sem + 3, sem + 2)
        plane_send(lambda q: v, vc.at[r], sem + 5, sem + 4)
        vr[c] = vs[ph]
        vc[r] = vs[ph]
        hooks[0]()

        @pl.when(zh == 0)
        def _():
            arrived(vc.at[other_r], sem)
            plane_send(lambda q: vc.at[other_r], vc.at[other_r], sem + 7, sem + 6)

        hooks[1]()
        arrived(vr.at[pl.ds(0, NCOL - 1)], sem + 2)
        if ph == 0:
            load.wait()
        products(vr, 0, False, half)
        if half:
            for q in range(PLANE):
                cp2[q] = jnp.concatenate([prefix[meta[3, q], 0:8], prefix[meta[3, q + PLANE], 0:8]], 0).astype(BF16)
            plane_send(lambda q: cp2.at[q], rs2.at[p], sem + 9, sem + 8)
            rs2[p] = cp2[p]
        else:
            for q in range(PLANE):
                cp1[q, 0] = prefix[meta[3, q]].astype(BF16)
                cp1[q, 1] = prefix[meta[3, q + PLANE]].astype(BF16)

            @pl.when(zh == 0)
            def _():
                plane_send(lambda q: cp1.at[q], rs1.at[p], sem + 9, sem + 8)

            @pl.when(zh == 1)
            def _():
                plane_send(lambda q: cp1.at[q, 1], rs1.at[p, 1], sem + 9, sem + 8)

            rs1[p] = cp1[p]

        arrived(vc.at[pl.ds(0, PLANE - 1)], sem + 4)

        @pl.when(zh == 0)
        def _():
            arrived(vc.at[pl.ds(0, PLANE - 1)], sem + 6)

        products(vc, 4, True, half)
        m = 8 if half else 16
        rp, cr = (rp2, cr2) if half else (rp1, cr1)
        for q in range(NCOL):
            rp[q] = prefix[meta[7, q], 0:m].astype(rp.dtype)
        col_send(lambda q: rp.at[q], cr.at[c], sem + 11, sem + 10)
        cr[c] = rp[c]
        hooks[2]()

        if half:
            arrived(rs2.at[pl.ds(0, PLANE - 1)], sem + 8)
            total = jnp.sum(rs2[...].astype(F32), axis=0)
            near, far = total[0:8], total[8:16]
        else:
            @pl.when(zh == 0)
            def _():
                arrived(rs1.at[pl.ds(0, PLANE - 1)], sem + 8)

            @pl.when(zh == 1)
            def _():
                arrived(rs1.at[pl.ds(0, PLANE - 1), 1], sem + 8)

            far = jnp.sum(rs1[:, 1].astype(F32), axis=0)

        z_out, z_in = zs.at[ph, pl.ds(0, m)], zr.at[ph, pl.ds(0, m)]
        zs[ph, 0:m] = far

        @pl.when(zh == 0)
        def _():
            copy(z_out, z_in, sem + 13, sem + 12, (other_r, c)).start()
            if half:
                zr[ph, 0:m] = near
            else:
                zr[ph, 0:m] = jnp.sum(rs1[:, 0].astype(F32), axis=0)

        hooks[3]()
        arrived(cr.at[pl.ds(0, NCOL - 1)], sem + 10)
        total = jnp.sum(cr[...].astype(F32), axis=0)

        @pl.when(zh == 1)
        def _():
            arrived(z_in, sem + 12)

        result = total + zr[ph, 0:m] + jnp.where(zh == 1, 1.0, 0.0) * zs[ph, 0:m]

        def drain():
            left(vr.at[pl.ds(0, NCOL - 1)], sem + 3)
            left(vc.at[pl.ds(0, PLANE - 1)], sem + 5)
            left(rp.at[pl.ds(0, NCOL - 1)], sem + 11)
            if half:
                left(cp2.at[pl.ds(0, PLANE - 1)], sem + 9)

            @pl.when(zh == 0)
            def _():
                left(vc.at[pl.ds(0, PLANE - 1)], sem + 7)
                if not half:
                    left(cp1.at[pl.ds(0, PLANE - 1)], sem + 9)
                left(z_out, sem + 13)

            @pl.when(zh == 1)
            def _():
                left(vs.at[ph], sem + 1)
                if not half:
                    left(cp1.at[pl.ds(0, PLANE - 1), 1], sem + 9)

        return result, drain

    def reduce_steps(k, sem):
        def first(tile):
            gs[k] = tile
            copy(gs.at[k], gr.at[k], sem + 1, sem, (r, other_core)).start()

        def second():
            arrived(gr.at[k], sem)
            gp[k, p] = gs[k] + gr[k]
            plane_send(lambda q: gp.at[k, p], gp.at[k, p], sem + 3, sem + 2)

        def third():
            arrived(gp.at[k, pl.ds(0, PLANE - 1)], sem + 2)
            gz[k, zi] = jnp.sum(gp[k], axis=0)
            z_send(gz.at[k, zi], gz.at[k, zi], sem + 5, sem + 4)

        def fourth():
            arrived(gz.at[k, pl.ds(0, ZALL - 1)], sem + 4)
            return jnp.sum(gz[k], axis=0)

        def drain():
            left(gs.at[k], sem + 1)
            left(gp.at[k, pl.ds(0, PLANE - 1)], sem + 3)
            left(gz.at[k, pl.ds(0, ZALL - 1)], sem + 5)

        return first, second, third, fourth, drain

    def nothing():
        return None

    both, drain1 = apply_h(0, 2, [nothing] * 4)
    hx, hp = both[0:8], both[8:16]
    high = hx.astype(BF16)
    vs[1] = jnp.concatenate([hx, hx - high.astype(F32)], 0).astype(BF16)
    first, second, third, fourth, drain3 = reduce_steps(0, 30)
    basis = jnp.concatenate([x, d, hx], 0)
    early = {}

    def hook0():
        first(gram_tile(basis))

    def hook3():
        rot, scale = rotation(turn_ref[0, 0], turn_ref[0, 1], fourth())
        early["xp"] = dot(rot[:, 0:24], basis, ((1,), (0,)), HI) * scale
        early["rot"], early["scale"] = rot, scale

    hhx, drain2 = apply_h(1, 16, [hook0, second, third, hook3])
    xp, rot, scale = early["xp"], early["rot"], early["scale"]
    image = dot(rot[0:8, 0:24], jnp.concatenate([hx, hp, hhx], 0), ((1,), (0,)), HI) * scale[0:8]
    basis2 = jnp.concatenate([xp, image], 0)
    first, second, third, fourth, drain4 = reduce_steps(1, 36)
    first(gram_tile(basis2))
    second()
    third()
    drain1()
    drain2()
    drain3()
    rot2, scale2 = rotation(turn_ref[1, 0], turn_ref[1, 1], fourth())
    o_ref[...] = dot(rot2[0:8, 0:24], basis2, ((1,), (0,)), HI) * scale2[0:8]
    drain4()


def body(x_start, p_start, blocks, block_in_row, col_block, coefs):
    vmem = pl.BlockSpec(memory_space=pltpu.VMEM)
    meta, turn = pl.pallas_call(
        prepare,
        out_shape=(jax.ShapeDtypeStruct((8, 128), jnp.int32), jax.ShapeDtypeStruct((2, 2, 8, 128), F32)),
        in_specs=[vmem] * 3,
        out_specs=(vmem, vmem),
        scratch_shapes=[pltpu.VMEM((8, 128), F32)],
        name="prepare",
    )(block_in_row, col_block, coefs)
    return pl.pallas_call(
        kernel,
        out_shape=jax.ShapeDtypeStruct((8, 128), F32),
        in_specs=[vmem, vmem, pl.BlockSpec(memory_space=pl.ANY), pl.BlockSpec(memory_space=pltpu.SMEM), vmem],
        out_specs=vmem,
        scratch_shapes=[
            pltpu.VMEM((NNZ, 128, 128), BF16),
            pltpu.VMEM((2, 16, 128), BF16),
            pltpu.VMEM((NCOL, 16, 128), BF16),
            pltpu.VMEM((NCOL, 16, 128), BF16),
            pltpu.VMEM((2 * PLANE, 16, 128), BF16),
            pltpu.VMEM((2 * PLANE, 16, 128), BF16),
            pltpu.VMEM((NNZ + 1, 16, 128), F32),
            pltpu.VMEM((PLANE, 2, 16, 128), BF16),
            pltpu.VMEM((PLANE, 16, 128), BF16),
            pltpu.VMEM((NCOL, 16, 128), BF16),
            pltpu.VMEM((NCOL, 8, 128), F32),
            pltpu.VMEM((PLANE, 2, 16, 128), BF16),
            pltpu.VMEM((PLANE, 16, 128), BF16),
            pltpu.VMEM((NCOL, 16, 128), BF16),
            pltpu.VMEM((NCOL, 8, 128), F32),
            pltpu.VMEM((2, 16, 128), F32),
            pltpu.VMEM((2, 16, 128), F32),
            pltpu.VMEM((2, 8, 128), F32),
            pltpu.VMEM((2, 8, 128), F32),
            pltpu.VMEM((2, PLANE, 8, 128), F32),
            pltpu.VMEM((2, ZALL, 8, 128), F32),
            pltpu.SemaphoreType.DMA((NSEM,)),
        ],
        compiler_params=pltpu.CompilerParams(
            collective_id=0, has_side_effects=True, vmem_limit_bytes=32 * 1024 * 1024
        ),
        name="lobpcg",
    )(x_start, p_start, blocks, meta, turn)


def solution(mesh):
    return jax.shard_map(
        body,
        mesh=mesh,
        in_specs=(
            P(None, ("row", "col")),
            P(None, ("row", "col")),
            P("row", "col", None, None, None),
            P("row", "col", None),
            P("row", "col", None),
            P(),
        ),
        out_specs=P(None, ("row", "col")),
        check_vma=False,
    )
```

time: 2430 us -> 103 us (0.04)
  blocking collectives: 1250 us -> 0 us
  waiting for transfers between devices: 1150 us -> 0 us
  Pallas kernels: 0 us -> 96.4 us
    reduce_scatter x4 -> x0, waiting for transfers between devices: 1140 us -> none  [the longest x2 1090 us: apply_h(): lower = lax.psum_scatter(col_part, 'row', scatter_dimension=1, tiled=True)]
    all_gather x4 -> x0, blocking collectives: 644 us -> none  [the longest x2 555 us: apply_h(): lax.all_gather(low, 'row', axis=1, tiled=True).reshape(rows, -1, BLOCK)]
    psum x4 -> x0, blocking collectives: 601 us -> none  [the longest x2 339 us: body(): quot = lax.psum(upper_products(present_states, hx.T), ('row', 'col'))]
    pallas_call x0 -> x2, Pallas kernels: none -> 96.4 us  [the longest x1 94.6 us: body(): pl.pallas_call(kernel, out_shape=jax.ShapeDtypeStruct((8, 128), F32), in_...]
  transfers between devices with their start and end apart: 4 -> 0, of which waited for: 3 -> 0; matrix products, arithmetic and copies ran while one was open for 0% -> 0% of each run, Pallas kernels for 0% -> 0%
where the time goes in v1:
time: 103 us
  Pallas kernels  96.4 us (94%)
  local copies, waits for them, and re-layouts  6.64 us (6%)
    pallas_call x1, Pallas kernels, body(): pl.pallas_call(kernel, out_shape=jax.ShapeDtypeStruct((8, 128), F32), in_...  94.6 us
    unnamed x12, local copies, waits for them, and re-layouts  6.64 us

profile of v1, /device:TPU:1, one launch (start us, length us, event | category | flops | bytes accessed | tf_op | source)
XLA Modules:
  0.0 103.0 jit_solution(5183089252824990209)
XLA Ops:
  0.0 1.4 %copy.7.coef_ref = f32[2,24,8]{2,1,0:T(8,128)} copy(f32[2,24,8]{1,2,0:T(8,128)} %param.11) | data formatting | bytes 3072 | tf_op args[5]
  1.4 1.8 %prepare.1 = (s32[8,128]{1,0:T(8,128)}, f32[2,2,8,128]{3,2,1,0:T(8,128)}) custom-call(s32[1,1,96]{2,1,0:T(1,128)} %row_ref.1, s32[1,1,96]{2,1,0:T(1,128)} %col_ref.1, f32[2,24,8]{2,1,0:T(8,128)} %copy.7.coef_ref), custom_call_target="tpu_custom_call" | custom-call | tf_op jit(solution)/shard_map/prepare/pallas_call | solution.py:358
  3.2 0.0 copy-start
  3.2 1.9 %copy-done = bf16[1,1,96,128,128]{4,3,2,1,0:T(8,128)(2,1)S(1)} copy-done((bf16[1,1,96,128,128]{4,3,2,1,0:T(8,128)(2,1)S(1)}, bf16[1,1,96,128,128]{4,3,2,1,0:T(8,128)(2,1)}, u32[]{:S(2)}) %copy-start) | copy-done | bytes 3145752
  5.1 0.0 copy-start.1
  5.1 0.7 copy-done.1
  5.8 0.0 copy-start.2
  5.8 0.7 copy-done.2
  6.5 0.0 copy-start.3
  6.5 0.7 copy-done.3
  7.2 0.0 copy-start.4
  7.2 0.7 copy-done.4
  7.8 94.6 %lobpcg.1 = f32[8,128]{1,0:T(8,128)S(1)} custom-call(f32[8,128]{1,0:T(8,128)S(1)} %copy-done.2, f32[8,128]{1,0:T(8,128)S(1)} %copy-done.3, bf16[1,1,96,128,128]{4,3,2,1,0:T(8,128)(2,1)S(1)} %copy-done, s32[8,128]{1,0:T(8,128)S(1)} %copy-done.4, f32[2,2,8,128]{3,2,1,0:T(8,128)S(1)} %copy-done.1), custom_call_target="tpu_custom_call" | custom-call | tf_op jit(solution)/shard_map/lobpcg/pallas_call | solution.py:366
  102.4 0.6 copy.9
Async XLA Ops:
  3.2 1.9 %copy-start = (bf16[1,1,96,128,128]{4,3,2,1,0:T(8,128)(2,1)S(1)}, bf16[1,1,96,128,128]{4,3,2,1,0:T(8,128)(2,1)}, u32[]{:S(2)}) copy-start(bf16[1,1,96,128,128]{4,3,2,1,0:T(8,128)(2,1)} %blk_hbm.1) | copy-start | bytes 9437188
  5.1 0.7 copy-start.1
  5.8 0.7 copy-start.2
  6.5 0.7 copy-start.3
  7.2 0.7 copy-start.4

commit v2 on v1

v2 whole, which is shorter than its diff:
```python
import jax
import jax.numpy as jnp
from jax import lax
from jax.experimental import pallas as pl
from jax.experimental.pallas import tpu as pltpu
from jax.sharding import PartitionSpec as P

MESH = pl.DeviceIdType.MESH
HI = lax.Precision.HIGHEST
F32, BF16 = jnp.float32, jnp.bfloat16
NNZ = 96
PLANE = 32
NCOL = 16
ZLOW = NCOL // 2
ZALL = 2 * ZLOW
UNROLL = 48
NSEM = 52


def dot(a, b, dims, precision=None):
    return lax.dot_general(a, b, (dims, ((), ())), precision=precision, preferred_element_type=F32)


def sort_meta(key_row, other_row, pad_ref):
    lane = lax.broadcasted_iota(jnp.int32, (128, 128), 1)
    sub = lax.broadcasted_iota(jnp.int32, (128, 128), 0)
    pad_ref[...] = jnp.full((8, 128), 1000, jnp.int32)
    pad_ref[0:1, 0:NNZ] = key_row
    pad_ref[1:2, 0:NNZ] = other_row
    key_lane = jnp.broadcast_to(pad_ref[0:1, :], (128, 128))
    other_lane = jnp.broadcast_to(pad_ref[1:2, :], (128, 128))
    key_sub = key_lane.T
    other_sub = other_lane.T
    before = (key_lane < key_sub) | ((key_lane == key_sub) & (lane < sub))
    rank = jnp.sum(jnp.where(before, 1, 0), axis=1, keepdims=True)
    here = rank == lane
    place = jnp.sum(jnp.where(here, sub, 0), axis=0, keepdims=True)
    other = jnp.sum(jnp.where(here, other_sub, 0), axis=0, keepdims=True)
    key = jnp.sum(jnp.where(here, key_sub, 0), axis=0, keepdims=True)
    earlier = jnp.sum(jnp.where(rank == lane - 1, key_sub, 0), axis=0, keepdims=True)
    keep = jnp.where(key == earlier, 1, 0)
    end = jnp.sum(jnp.where(key_sub <= lane, 1, 0), axis=0, keepdims=True)
    start = jnp.sum(jnp.where(key_sub < lane, 1, 0), axis=0, keepdims=True)
    last = jnp.where(end > start, end, 0)
    return place, other, keep, last


SHIFTS = (0, 32, 56, 72, 80)


def gram_tile(basis):
    padded = jnp.concatenate([basis, jnp.zeros((88, 128), F32)], 0)
    g = dot(basis, padded, ((1,), (1,)), HI)
    lane = lax.broadcasted_iota(jnp.int32, (8, 128), 1)
    tile = g[0:8]
    for i in range(1, 5):
        tile += pltpu.roll(jnp.where(lane >= 8 * i, g[8 * i:8 * i + 8], 0.0), SHIFTS[i], 1)
    return tile


def gram_full(tile):
    lane = lax.broadcasted_iota(jnp.int32, (8, 128), 1)
    upper, strict = [], []
    for i in range(5):
        part = tile if i == 0 else pltpu.roll(tile, 128 - SHIFTS[i], 1)
        upper.append(jnp.where((lane >= 8 * i) & (lane < 40), part, 0.0))
        strict.append(jnp.where((lane >= 8 * i + 8) & (lane < 40), part, 0.0))
    rest = [jnp.zeros((88, 128), F32)]
    return jnp.concatenate(upper + rest, 0) + jnp.concatenate(strict + rest, 0).T


def turns(coef_t):
    k = lax.broadcasted_iota(jnp.int32, (24, 128), 0)
    lane = lax.broadcasted_iota(jnp.int32, (24, 128), 1)
    place = jnp.where(k < 8, k, jnp.where(k < 16, k + 8, k - 8))
    only = (lane == k - 8) & (k >= 8) & (k < 16)
    ct = dot(coef_t, jnp.where(lane == place, 1.0, 0.0).astype(F32), ((1,), (0,)), HI)
    cb = dot(coef_t, jnp.where(only, 1.0, 0.0).astype(F32), ((1,), (0,)), HI)
    return ct, cb


def rotation(turn, gram):
    ct, cb = turn
    lane = lax.broadcasted_iota(jnp.int32, (8, 128), 1)
    at = jnp.where(lane < 8, gram[16:24], 0.0)
    back = dot(cb[:, 0:8], at, ((1,), (0,)), HI)
    both = jnp.concatenate([ct - back, jnp.where(lane < 8, 0.0, ct) - back], 0)
    norm = jnp.sum(dot(both[:, 0:24], gram[0:24], ((1,), (0,)), HI) * both, axis=1, keepdims=True)
    return both, 1.0 / jnp.sqrt(norm)


def kernel(x_hbm, p_hbm, blk_hbm, row_hbm, col_hbm, coef_hbm, o_ref,
           x_ref, p_ref, coef_ref, row_ref, col_ref, pad, meta_v, meta, blk, vs, vr1, vr2, vc1, vc2, prefix, cp1, cp2, rp1, rp2, sb1, sb2, st1, st2, rs1, rs2, cr1, cr2, zs, zr,
           gs, gr, gp, gz, sems):
    r = lax.axis_index("row")
    c = lax.axis_index("col")
    zh = r // PLANE
    p = lax.rem(r, PLANE)
    zl = c // 2
    core = lax.rem(c, 2)
    zi = zh * ZLOW + zl
    ci = core * ZLOW + zl
    mine = pl.ds(core * ZLOW, ZLOW)
    others = pl.ds((1 - core) * ZLOW, ZLOW)
    other_core = zl * 2 + 1 - core
    other_r = (1 - zh) * PLANE + p

    def copy(src, dst, send, recv, dev):
        return pltpu.make_async_remote_copy(
            src_ref=src, dst_ref=dst, send_sem=sems.at[send], recv_sem=sems.at[recv], device_id=dev, device_id_type=MESH
        )

    def arrived(ref, sem):
        copy(ref, ref, NSEM - 1, sem, (r, other_core)).wait_recv()

    def left(ref, sem):
        copy(ref, ref, sem, NSEM - 1, (r, other_core)).wait_send()

    def plane_send(src, dst, send, recv):
        def step(i, _):
            q = lax.rem(p + i, PLANE)
            copy(src(q), dst, send, recv, (zh * PLANE + q, c)).start()
            return 0

        lax.fori_loop(1, PLANE, step, 0)

    def col_send(src, dst, send, recv):
        def step(i, _):
            q = lax.rem(zl + i, ZLOW)
            copy(src(q), dst, send, recv, (r, q * 2 + core)).start()
            return 0

        lax.fori_loop(1, ZLOW, step, 0)

    def z_send(src, dst, send, recv):
        def step(i, _):
            q = lax.rem(zi + i, ZALL)
            copy(src, dst, send, recv, (q // ZLOW * PLANE + p, lax.rem(q, ZLOW) * 2 + core)).start()
            return 0

        lax.fori_loop(1, ZALL, step, 0)

    bar = pltpu.get_barrier_semaphore()

    def greet_plane(i, _):
        pl.semaphore_signal(bar, 1, device_id=(zh * PLANE + lax.rem(p + i, PLANE), c), device_id_type=MESH)
        return 0

    def greet_col(i, _):
        pl.semaphore_signal(bar, 1, device_id=(r, lax.rem(zl + i, ZLOW) * 2 + core), device_id_type=MESH)
        return 0

    def greet_far(i, _):
        pl.semaphore_signal(bar, 1, device_id=(other_r, i * 2 + core), device_id_type=MESH)
        return 0

    lax.fori_loop(0, ZLOW, greet_far, 0)
    lax.fori_loop(1, ZLOW, greet_col, 0)
    pl.semaphore_signal(bar, 1, device_id=(r, other_core), device_id_type=MESH)
    lax.fori_loop(1, PLANE, greet_plane, 0)

    small = [
        pltpu.make_async_copy(src, dst, sems.at[n])
        for src, dst, n in (
            (row_hbm, row_ref, 49), (col_hbm, col_ref, 50), (x_hbm, x_ref, 1), (p_hbm, p_ref, 46), (coef_hbm, coef_ref, 47)
        )
    ]
    for one in small:
        one.start()
    load = pltpu.make_async_copy(blk_hbm.at[0, 0], blk, sems.at[0])
    load.start()
    for one in small:
        one.wait()
    x = x_ref[...]
    d = p_ref[...]
    vs[0] = jnp.concatenate([x, d], 0).astype(BF16)

    @pl.when(zh == 1)
    def _():
        vc1[0:PLANE] = jnp.zeros((PLANE, 16, 128), BF16)
        vc2[0:PLANE] = jnp.zeros((PLANE, 16, 128), BF16)

    prefix[0] = jnp.zeros((16, 128), F32)
    rows = row_ref[0]
    rows = lax.rem(rows, 2) * ZLOW + rows // 2
    cols = col_ref[0]
    for i, v in enumerate(sort_meta(cols, rows, pad) + sort_meta(rows, cols, pad)):
        meta_v[i:i + 1, :] = v
    tables = pltpu.make_async_copy(meta_v, meta, sems.at[48])
    tables.start()
    tables.wait()
    turn1, turn2 = turns(coef_ref[0]), turns(coef_ref[1])
    pl.semaphore_wait(bar, PLANE - 1 + ZLOW - 1 + 1 + ZLOW)

    def products(v_ref, base, transposed, half):
        dims = ((1,), (1,)) if transposed else ((1,), (0,))
        m = 8 if half else 16

        def step(it, total):
            for u in range(UNROLL):
                k = it * UNROLL + u
                part = dot(v_ref[meta[base + 1, k]], blk[meta[base, k]], dims)
                if half:
                    part = part[0:8] + part[8:16]
                total = total * meta[base + 2, k].astype(F32) + part
                prefix[k + 1, 0:m] = total
            return total

        lax.fori_loop(0, NNZ // UNROLL, step, jnp.zeros((m, 128), F32))

    def apply_h(ph, sem):
        half = ph == 1
        v = vs.at[ph]
        vr, vc = (vr2, vc2) if half else (vr1, vc1)

        @pl.when(zh == 1)
        def _():
            copy(v, vc.at[r], sem + 1, sem, (p, c)).start()

        col_send(lambda q: v, vr.at[ci], sem + 3, sem + 2)
        plane_send(lambda q: v, vc.at[r], sem + 5, sem + 4)
        vr[ci] = vs[ph]
        vc[r] = vs[ph]
        arrived(vr.at[pl.ds(0, ZLOW - 1)], sem + 2)
        copy(vr.at[mine], vr.at[mine], sem + 15, sem + 14, (r, other_core)).start()

        @pl.when(zh == 0)
        def _():
            arrived(vc.at[other_r], sem)
            plane_send(lambda q: vc.at[other_r], vc.at[other_r], sem + 7, sem + 6)

        arrived(vr.at[others], sem + 14)
        if ph == 0:
            load.wait()
        products(vr, 0, False, half)
        if half:
            for q in range(PLANE):
                cp2[q] = jnp.concatenate([prefix[meta[3, q], 0:8], prefix[meta[3, q + PLANE], 0:8]], 0).astype(BF16)
            plane_send(lambda q: cp2.at[q], rs2.at[p], sem + 9, sem + 8)
            rs2[p] = cp2[p]
        else:
            for q in range(PLANE):
                cp1[q, 0] = prefix[meta[3, q]]
                cp1[q, 1] = prefix[meta[3, q + PLANE]]

            plane_send(lambda q: cp1.at[q, 1], rs1.at[p, 1], sem + 9, sem + 8)
            rs1[p] = cp1[p]

        arrived(vc.at[pl.ds(0, PLANE - 1)], sem + 4)

        @pl.when(zh == 0)
        def _():
            arrived(vc.at[pl.ds(0, PLANE - 1)], sem + 6)

        products(vc, 4, True, half)
        m = 8 if half else 16
        rp, sb, st, cr = (rp2, sb2, st2, cr2) if half else (rp1, sb1, st1, cr1)
        for q in range(NCOL):
            rp[q] = prefix[meta[7, q], 0:m]
        copy(rp.at[others], sb, sem + 17, sem + 16, (r, other_core)).start()
        arrived(sb, sem + 16)
        st[...] = (rp[mine] + sb[...]).astype(st.dtype)
        col_send(lambda q: st.at[q], cr.at[zl], sem + 11, sem + 10)
        cr[zl] = st[zl]
        if not half:
            @pl.when(zh == 0)
            def _():
                plane_send(lambda q: cp1.at[q, 0], rs1.at[p, 0], 45, 44)


        if half:
            arrived(rs2.at[pl.ds(0, PLANE - 1)], sem + 8)
            total = jnp.sum(rs2[...].astype(F32), axis=0)
            near, far = total[0:8], total[8:16]
        else:
            arrived(rs1.at[pl.ds(0, PLANE - 1), 1], sem + 8)
            far = jnp.sum(rs1[:, 1].astype(F32), axis=0)

        z_out, z_in = zs.at[ph, pl.ds(0, m)], zr.at[ph, pl.ds(0, m)]
        zs[ph, 0:m] = far

        @pl.when(zh == 0)
        def _():
            copy(z_out, z_in, sem + 13, sem + 12, (other_r, c)).start()
            if half:
                zr[ph, 0:m] = near
            else:
                arrived(rs1.at[pl.ds(0, PLANE - 1), 0], 44)
                zr[ph, 0:m] = jnp.sum(rs1[:, 0].astype(F32), axis=0)

        arrived(cr.at[pl.ds(0, ZLOW - 1)], sem + 10)
        total = jnp.sum(cr[...].astype(F32), axis=0)

        @pl.when(zh == 1)
        def _():
            arrived(z_in, sem + 12)

        result = total + zr[ph, 0:m] + jnp.where(zh == 1, 1.0, 0.0) * zs[ph, 0:m]

        def drain():
            left(vr.at[pl.ds(0, ZLOW - 1)], sem + 3)
            left(vr.at[mine], sem + 15)
            left(sb, sem + 17)
            left(vc.at[pl.ds(0, PLANE - 1)], sem + 5)
            left(st.at[pl.ds(0, ZLOW - 1)], sem + 11)
            left(cp2.at[pl.ds(0, PLANE - 1)] if half else cp1.at[pl.ds(0, PLANE - 1), 1], sem + 9)

            @pl.when(zh == 0)
            def _():
                left(vc.at[pl.ds(0, PLANE - 1)], sem + 7)
                if not half:
                    left(cp1.at[pl.ds(0, PLANE - 1), 0], 45)
                left(z_out, sem + 13)

            @pl.when(zh == 1)
            def _():
                left(vs.at[ph], sem + 1)

        return result, drain

    both, drain1 = apply_h(0, 2)
    hx, hp = both[0:8], both[8:16]
    high = hx.astype(BF16)
    vs[1] = jnp.concatenate([hx, hx - high.astype(F32)], 0).astype(BF16)
    hhx, drain2 = apply_h(1, 20)

    basis = jnp.concatenate([x, d, hx, hp, hhx], 0)
    gs[...] = gram_tile(basis)
    copy(gs, gr, 39, 38, (r, other_core)).start()
    arrived(gr, 38)
    gp[p] = gs[...] + gr[...]
    plane_send(lambda q: gp.at[p], gp.at[p], 41, 40)
    arrived(gp.at[pl.ds(0, PLANE - 1)], 40)
    gz[zi] = jnp.sum(gp[...], axis=0)
    z_send(gz.at[zi], gz.at[zi], 43, 42)
    drain1()
    drain2()
    left(gs, 39)
    left(gp.at[pl.ds(0, PLANE - 1)], 41)
    arrived(gz.at[pl.ds(0, ZALL - 1)], 42)
    gram = gram_full(jnp.sum(gz[...], axis=0))

    rot, scale = rotation(turn1, gram)
    new = rot * scale
    new = jnp.concatenate([new, pltpu.roll(new[0:8], 16, 1)], 0)
    padded = jnp.concatenate([new, jnp.zeros((104, 128), F32)], 0)
    gram2 = dot(dot(new, gram, ((1,), (0,)), HI), padded, ((1,), (1,)), HI)
    rot2, scale2 = rotation(turn2, gram2)
    final = dot(rot2[0:8, 0:24], new, ((1,), (0,)), HI) * scale2[0:8]
    o_ref[...] = dot(final[:, 0:40], basis, ((1,), (0,)), HI)
    left(gz.at[pl.ds(0, ZALL - 1)], 43)


def body(x_start, p_start, blocks, block_in_row, col_block, coefs):
    vmem = pl.BlockSpec(memory_space=pltpu.VMEM)
    hbm = pl.BlockSpec(memory_space=pltpu.HBM)
    limit = 56 * 1024 * 1024
    return pl.pallas_call(
        kernel,
        out_shape=jax.ShapeDtypeStruct((8, 128), F32),
        in_specs=[hbm] * 6,
        out_specs=vmem,
        scratch_shapes=[
            pltpu.VMEM((8, 128), F32),
            pltpu.VMEM((8, 128), F32),
            pltpu.VMEM((2, 8, 24), F32),
            pltpu.VMEM((1, 1, NNZ), jnp.int32),
            pltpu.VMEM((1, 1, NNZ), jnp.int32),
            pltpu.VMEM((8, 128), jnp.int32),
            pltpu.VMEM((8, 128), jnp.int32),
            pltpu.SMEM((8, 128), jnp.int32),
            pltpu.VMEM((NNZ, 128, 128), BF16),
            pltpu.VMEM((2, 16, 128), BF16),
            pltpu.VMEM((NCOL, 16, 128), BF16),
            pltpu.VMEM((NCOL, 16, 128), BF16),
            pltpu.VMEM((2 * PLANE, 16, 128), BF16),
            pltpu.VMEM((2 * PLANE, 16, 128), BF16),
            pltpu.VMEM((NNZ + 1, 16, 128), F32),
            pltpu.VMEM((PLANE, 2, 16, 128), F32),
            pltpu.VMEM((PLANE, 16, 128), BF16),
            pltpu.VMEM((NCOL, 16, 128), F32),
            pltpu.VMEM((NCOL, 8, 128), F32),
            pltpu.VMEM((ZLOW, 16, 128), F32),
            pltpu.VMEM((ZLOW, 8, 128), F32),
            pltpu.VMEM((ZLOW, 16, 128), F32),
            pltpu.VMEM((ZLOW, 8, 128), F32),
            pltpu.VMEM((PLANE, 2, 16, 128), F32),
            pltpu.VMEM((PLANE, 16, 128), BF16),
            pltpu.VMEM((ZLOW, 16, 128), F32),
            pltpu.VMEM((ZLOW, 8, 128), F32),
            pltpu.VMEM((2, 16, 128), F32),
            pltpu.VMEM((2, 16, 128), F32),
            pltpu.VMEM((8, 128), F32),
            pltpu.VMEM((8, 128), F32),
            pltpu.VMEM((PLANE, 8, 128), F32),
            pltpu.VMEM((ZALL, 8, 128), F32),
            pltpu.SemaphoreType.DMA((NSEM,)),
        ],
        compiler_params=pltpu.CompilerParams(
            collective_id=0, has_side_effects=True, vmem_limit_bytes=limit
        ),
        name="lobpcg",
    )(x_start, p_start, blocks, block_in_row, col_block, jnp.transpose(coefs, (0, 2, 1)))


def solution(mesh):
    return jax.shard_map(
        body,
        mesh=mesh,
        in_specs=(
            P(None, ("row", "col")),
            P(None, ("row", "col")),
            P("row", "col", None, None, None),
            P("row", "col", None),
            P("row", "col", None),
            P(),
        ),
        out_specs=P(None, ("row", "col")),
        check_vma=False,
    )
```

time: 103 us -> 94.1 us (0.914)
  local copies, waits for them, and re-layouts: 6.64 us -> 1.28 us
  Pallas kernels: 96.4 us -> 92.5 us
    unnamed x12 -> x1, local copies, waits for them, and re-layouts: 6.64 us -> 1.28 us
    pallas_call x1, Pallas kernels: 94.6 us -> 92.5 us  [body(): pl.pallas_call(kernel, out_shape=jax.ShapeDtypeStruct((8, 128), F32), in_...]
    pallas_call x1 -> x0, Pallas kernels: 1.79 us -> none  [body(): pl.pallas_call(prepare, out_shape=(jax.ShapeDtypeStruct((8, 128), jnp.int...]
where the time goes in v2:
time: 94.1 us; the launch traced here: 93.8 us
  Pallas kernels  92.5 us (98%)
  local copies, waits for them, and re-layouts  1.28 us (1%)
    pallas_call x1, Pallas kernels, body(): pl.pallas_call(kernel, out_shape=jax.ShapeDtypeStruct((8, 128), F32), in_...  92.5 us

profile of v2, /device:TPU:1, one launch (start us, length us, event | category | flops | bytes accessed | tf_op | source)
XLA Modules:
  0.0 93.8 jit_solution(1932953390144133636)
XLA Ops:
  0.0 92.5 %lobpcg.1 = f32[8,128]{1,0:T(8,128)} custom-call(f32[8,128]{1,0:T(8,128)} %x_hbm.1, f32[8,128]{1,0:T(8,128)} %p_hbm.1, bf16[1,1,96,128,128]{4,3,2,1,0:T(8,128)(2,1)} %blk_hbm.1, s32[1,1,96]{2,1,0:T(1,128)} %row_hbm.1, s32[1,1,96]{2,1,0:T(1,128)} %col_hbm.1, f32[2,8,24]{2,1,0:T(8,128)} %bitcast.1), custom_call_target="tpu_custom_call" | custom-call | tf_op jit(solution)/shard_map/lobpcg/pallas_call | solution.py:358
  92.6 1.3 %copy.8 = f32[8,128]{1,0:T(8,128)} copy(f32[8,128]{1,0:T(8,128)} %lobpcg.1) | data formatting | bytes 8192
